TPU v7x, 256 devices: a whole 4x4x8 slice. The times are simulated.
256 devices in a mesh: ctx: 32 (over z, x_lo, core), tp: 8 (over x_hi, y).
Axes of the slice: x: 4 (x_hi: 2, x_lo: 2; x = x_hi * 2 + x_lo), y: 4, z: 8, core: 2. Of those that a mesh axis runs over, the one named last changes fastest.
Arguments:
- projected: bfloat16 [8192, 3, 8192], P('ctx', None, 'tp'), may hold values from -6 to 6
- cotangent: bfloat16 [8192, 8192], P('ctx', 'tp')
- short_filter: float32 [7, 3, 8192], P(None, None, 'tp'), may hold values from -2 to 2
- long_filter: float32 [128, 8192], P(None, 'tp'), may hold values from -0.5 to 0.5
Outputs:
- scaled_grad: bfloat16 [8192, 3, 8192], P('ctx', None, 'tp')
- long_grad: float32 [128, 8192], P('ctx', 'tp')
- short_grad: float32 [7, 3, 8192], P(None, None, 'tp')
- grad_scale: float32 [], replicated
All inputs are finite; a program needn't handle non-finite values.
Results may differ from a plain program's by a relative error of at most 0.0017.
Values may be sent and summed in bfloat16 or wider, within the bound.
A program may use at most 128 MiB of HBM per device.

v0:
```python
import jax
import jax.numpy as jnp
from jax import lax
from jax.sharding import PartitionSpec as P

EPSILON = 1e-06
FP8_RANGE = 448.0


def shifted(value, axis, steps):
    count = lax.axis_size(axis)
    leading, last = (max(0, -steps), min(count, count - steps))
    return lax.ppermute(value, axis, [(source, source + steps) for source in range(leading, last)])


def as_sent(array):
    return jax.tree.map(lambda a: a.astype(jnp.bfloat16) if a.dtype == jnp.float32 else a, array)


def causal_filter(extended, kernel):
    operand = extended[None]
    kernel_in = kernel[::-1][:, None, :]
    result = lax.conv_general_dilated(
        operand,
        kernel_in,
        (1,),
        "VALID",
        dimension_numbers=("NWC", "WIO", "NWC"),
        feature_group_count=extended.shape[1],
        precision=lax.Precision.HIGHEST,
    )
    return result[0]


def later_filter(extended, kernel):
    operand = extended[None]
    kernel_in = kernel[:, None, :]
    result = lax.conv_general_dilated(
        operand,
        kernel_in,
        (1,),
        "VALID",
        dimension_numbers=("NWC", "WIO", "NWC"),
        feature_group_count=extended.shape[1],
        precision=lax.Precision.HIGHEST,
    )
    return result[0]


def body(projected, cotangent, short_filter, long_filter):
    row_count, streams, chan_count = projected.shape
    width_all = streams * chan_count
    tap_count = long_filter.shape[0]
    short_count = short_filter.shape[0]
    reach_rows = tap_count + short_count - 2
    inputs = projected.reshape(row_count, width_all)
    short_rows = short_filter.reshape(short_count, width_all)
    gradient = cotangent.astype(jnp.float32)
    prior_rows = shifted(inputs[row_count - reach_rows :], "ctx", 1)
    extended = jnp.concatenate([prior_rows, inputs], axis=0).astype(jnp.float32)
    features = causal_filter(extended, short_rows)
    query_part = features[:, :chan_count]
    key_part = features[:, chan_count : 2 * chan_count]
    value_part = features[:, 2 * chan_count :]
    product = key_part * value_part
    filtered = causal_filter(product, long_filter)
    span_rows = filtered.shape[0]
    query_own = query_part[tap_count - 1 : tap_count - 1 + span_rows]
    d_query = gradient * filtered
    d_filtered = gradient * query_own
    after_rows = shifted(d_filtered[: tap_count - 1], "ctx", -1)
    d_product = later_filter(jnp.concatenate([d_filtered, after_rows], axis=0), long_filter)
    key_own = key_part[tap_count - 1 : tap_count - 1 + row_count]
    value_own = value_part[tap_count - 1 : tap_count - 1 + row_count]
    d_features = jnp.concatenate(
        [d_query[:row_count], d_product * value_own, d_product * key_own], axis=1
    )
    tail_rows = shifted(as_sent(d_features[: short_count - 1]), "ctx", -1)
    d_features = jnp.concatenate([d_features, tail_rows], axis=0)
    d_input = later_filter(d_features, short_rows)
    long_local = later_filter(product[: row_count + tap_count - 1], d_filtered[:row_count])[::-1]
    short_local = later_filter(
        extended[reach_rows - short_count + 1 : reach_rows + row_count], d_features[:row_count]
    )[::-1]
    local_peak = jnp.max(jnp.abs(d_input))
    share = tap_count // lax.axis_size("ctx")
    long_all, short_all = lax.psum((long_local, short_local), "ctx")
    long_grad = lax.dynamic_slice_in_dim(long_all, lax.axis_index("ctx") * share, share, 0)
    peak = lax.pmax(local_peak, ("ctx", "tp"))
    factor = FP8_RANGE / (peak + EPSILON)
    scaled_grad = (d_input * factor).astype(jnp.bfloat16).reshape(row_count, streams, chan_count)
    grad_scale = (peak + EPSILON) / FP8_RANGE
    return (scaled_grad, long_grad, short_all.reshape(short_count, streams, chan_count), grad_scale)


def solution(mesh):
    placed = (P("ctx", None, "tp"), P("ctx", "tp"), P(None, None, "tp"), P(None, "tp"))
    return jax.shard_map(
        body,
        mesh=mesh,
        in_specs=placed,
        out_specs=(P("ctx", None, "tp"), P("ctx", "tp"), P(None, None, "tp"), P()),
        check_vma=False,
    )
```

profile of v0, /device:TPU:1, one launch (start us, length us, event | category | flops | bytes accessed | tf_op | source)
XLA Modules:
  0.0 365.2 jit_solution(15331506724432419009)
XLA Ops:
  11.0 4.5 %collective-permute-start = (bf16[133,3072]{1,0:T(8,128)(2,1)}, bf16[133,3072]{1,0:T(8,128)(2,1)}, u32[]{:S(2)}, u32[]{:S(2)}) collective-permute-start(bf16[133,3072]{1,0:T(8,128)(2,1)} %bitcast.22), channel_id=1, source_target_pairs={{0,8},{8,16},{16,24},{24,32},{32,40},{40,48},{48,56},{56,64},{64,7... | collective-permute-start | bytes 2451464 | tf_op jit(solution)/shard_map/ppermute | solution.py:13
  16.9 4.7 %rev.13 = f32[128,1024]{1,0:T(8,128)} reverse(f32[128,1024]{1,0:T(8,128)} %param.7), dimensions={0} | reverse | bytes 1048576 | tf_op jit(solution)/shard_map/rev | solution.py:22
  21.6 3.6 collective-permute-done
  26.9 2.9 fusion.9
  29.8 4.6 %copy.49 = bf16[1,389,3072]{2,1,0:T(8,128)(2,1)} copy(bf16[1,389,3072]{1,2,0:T(8,128)(2,1)} %fusion.9) | data formatting | bytes 4780032
  34.4 3.3 pad.clone
  37.7 4.0 %reshape.29 = bf16[1,8,49,3072]{3,2,1,0:T(8,128)(2,1)} reshape(bf16[1,392,3072]{2,1,0:T(8,128)(2,1)} %pad.clone) | data formatting | bytes 4816896 | tf_op jit(solution)/shard_map/conv_general_dilated | solution.py:23
  41.7 3.1 copy.25
  44.9 2.5 convolution_select_fusion
  47.4 5.3 %copy.26 = f32[8,49,3072]{2,1,0:T(8,128)} copy(f32[8,49,3072]{2,0,1:T(8,128)S(1)} %convolution_select_fusion) | data formatting | bytes 9633792 | tf_op jit(solution)/shard_map/conv_general_dilated | solution.py:23
  52.7 5.4 %reshape.33 = f32[1,392,3072]{2,1,0:T(8,128)} reshape(f32[8,49,3072]{2,1,0:T(8,128)} %copy.26) | data formatting | bytes 9633792 | tf_op jit(solution)/shard_map/conv_general_dilated | solution.py:23
  58.1 2.9 slice_bitcast_fusion
  62.3 10.6 %fusion.29 = f32[1,256,1024]{2,0,1:T(1,128)S(1)} fusion(f32[1,383,1024]{2,1,0:T(8,128)S(1)} %fusion.22, f32[128,1,1024]{2,0,1:T(8,128)S(1)} %bitcast.54), kind=kOutput, calls=%fused_computation.43 | convolution fusion | flops 402653184 | bytes 3141632 | tf_op jit(solution)/shard_map/conv_general_dilated | solution.py:23
  76.2 11.3 %fusion.26 = f32[1,128,1024]{2,0,1:T(1,128)} fusion(f32[256,1,1024]{2,0,1:T(8,128)S(1)} %bitcast.49, f32[1,383,1024]{2,1,0:T(8,128)S(1)} %fusion.22), kind=kOutput, calls=%fused_computation.40 | convolution fusion | flops 402653184 | bytes 3141632 | tf_op jit(solution)/shard_map/conv_general_dilated | solution.py:38
  87.5 2.9 fusion.19
  90.4 8.9 %copy.39 = bf16[1,262,3072]{2,0,1:T(2,128)(2,1)} copy(bf16[1,262,3072]{1,2,0:T(8,128)(2,1)} %fusion.19) | data formatting | bytes 3219456 | tf_op jit(solution)/shard_map/broadcast_in_dim | solution.py:36
  100.6 2.7 rev.14
  104.4 10.6 %fusion.23 = f32[1,256,1024]{2,0,1:T(1,128)S(1)} fusion(f32[1,383,1024]{2,1,0:T(8,128)S(1)} %maximum_bitcast_fusion.1, f32[128,1,1024]{2,0,1:T(8,128)S(1)} %bitcast.53), kind=kOutput, calls=%fused_computation.33 | convolution fusion | flops 402653184 | bytes 3141632 | tf_op jit(solution)/shard_map/conv_general_dilated | solution.py:38
  119.6 8.6 %fusion.10 = f32[1,7,3072]{2,0,1:T(1,128)S(1)} fusion(bf16[1,262,3072]{2,0,1:T(2,128)(2,1)S(1)} %copy-done.6, f32[256,1,3072]{2,0,1:T(8,128)S(1)} %fusion.40), kind=kOutput, calls=%fused_computation.19 | convolution fusion | flops 66060288 | bytes 4841472 | tf_op jit(solution)/shard_map/conv_general_dilated | solution.py:38
  130.3 4.9 %reshape.36 = f32[1,8,33,3072]{3,0,2,1:T(1,128)} reshape(f32[1,264,3072]{2,1,0:T(8,128)S(1)} %pad.2) | data formatting | bytes 6488064 | tf_op jit(solution)/shard_map/conv_general_dilated | solution.py:38
  135.2 2.5 copy.32
  137.9 2.9 select_reduce_fusion
  140.8 82.3 %pmax.7 = f32[]{:T(128)} all-reduce(f32[]{:T(128)} %get-tuple-element.14), channel_id=1, replica_groups=mesh['ctx'=32,'tp'=8] {'ctx','tp'}, use_global_device_ids=true, to_apply=%region_1.0 | all-reduce | flops 1 | bytes 8 | tf_op jit(solution)/shard_map/pmax | solution.py:89
  230.5 123.8 %all-reduce.3.cloned.1.call-done = (f32[128,1024]{1,0:T(8,128)}, f32[7,3,1024]{2,1,0:T(4,128)}) async-done(((f32[128,1024]{1,0:T(8,128)}, f32[7,3,1024]{2,1,0:T(4,128)}), (f32[128,1024]{1,0:T(8,128)}, f32[7,3,1024]{2,1,0:T(4,128)})) %all-reduce.3.cloned.1.call-update) | async-done | bytes 610320 | tf_op jit(solution)/shard_map/psum | solution.py:87
  (68 shorter events, 30.1 us)
Async XLA Ops:
  7.2 347.1 %all-reduce.3.cloned.1.call-start = ((), (), s32[]{:S(2)}) async-start(), calls=%async_computation | async-start | bytes 1277952 | tf_op jit(solution)/shard_map/psum | solution.py:87
  8.6 7.0 %copy-start.5 = (bf16[256,3,1024]{2,0,1:T(8,128)(2,1)S(1)}, bf16[256,3,1024]{2,0,1:T(8,128)(2,1)}, u32[]{:S(2)}) copy-start(bf16[256,3,1024]{2,0,1:T(8,128)(2,1)} %param.4) | copy-start | bytes 4718596
  9.3 7.0 %copy-start.10 = (f32[7,3,1024]{2,0,1:T(8,128)S(1)}, f32[7,3,1024]{2,0,1:T(8,128)}, u32[]{:S(2)}) copy-start(f32[7,3,1024]{2,0,1:T(8,128)} %param.6) | copy-start | bytes 258052
  11.0 14.3 %collective-permute-start = (bf16[133,3072]{1,0:T(8,128)(2,1)}, bf16[133,3072]{1,0:T(8,128)(2,1)}, u32[]{:S(2)}, u32[]{:S(2)}) collective-permute-start(bf16[133,3072]{1,0:T(8,128)(2,1)} %bitcast.22), channel_id=1, source_target_pairs={{0,8},{8,16},{16,24},{24,32},{32,40},{40,48},{48,56},{56,64},{64,7... | collective-permute-start | bytes 2451464 | tf_op jit(solution)/shard_map/ppermute | solution.py:13
  26.9 2.9 copy-start.1
  41.7 3.2 copy-start.12
  60.9 12.0 %copy-start = (f32[383,3072]{1,0:T(8,128)}, f32[383,3072]{1,0:T(8,128)S(1)}, u32[]{:S(2)}) copy-start(f32[383,3072]{1,0:T(8,128)S(1)} %slice_bitcast_fusion) | copy-start | bytes 14118916
  60.9 1.4 copy-start.9
  62.3 10.6 %copy-start.7 = (bf16[256,1024]{1,0:T(8,128)(2,1)S(1)}, bf16[256,1024]{1,0:T(8,128)(2,1)}, u32[]{:S(2)}) copy-start(bf16[256,1024]{1,0:T(8,128)(2,1)} %param.5) | copy-start | bytes 1572868
  73.4 2.8 copy-start.3
  74.3 29.0 %collective-permute-start.1 = (f32[127,1024]{1,0:T(8,128)}, f32[127,1024]{1,0:T(8,128)}, u32[]{:S(2)}, u32[]{:S(2)}) collective-permute-start(f32[127,1024]{1,0:T(8,128)} %slice.54), channel_id=1, source_target_pairs={{8,0},{16,8},{24,16},{32,24},{40,32},{48,40},{56,48},{64,56},{72,6... | collective-permute-start | bytes 1560584 | tf_op jit(solution)/shard_map/ppermute | solution.py:13
  76.2 11.3 %copy-start.2 = (bf16[133,3072]{0,1:T(8,128)(2,1)S(1)}, bf16[133,3072]{0,1:T(8,128)(2,1)}, u32[]{:S(2)}) copy-start(bf16[133,3072]{0,1:T(8,128)(2,1)} %copy-done.1) | copy-start | bytes 2451460
  90.4 12.8 %copy-start.4 = (f32[256,1024]{1,0:T(8,128)S(1)}, f32[256,1024]{1,0:T(8,128)}, u32[]{:S(2)}) copy-start(f32[256,1024]{1,0:T(8,128)} %copy-done.3) | copy-start | bytes 3145732
  99.4 5.1 %copy-start.8 = (f32[128,1024]{1,0:T(8,128)S(1)}, f32[128,1024]{1,0:T(8,128)}, u32[]{:S(2)}) copy-start(f32[128,1024]{1,0:T(8,128)} %param.7) | copy-start | bytes 1572868
  117.3 2.3 copy-start.6
  117.6 12.0 %collective-permute-start.2 = (bf16[6,3072]{1,0:T(8,128)(2,1)S(1)}, bf16[6,3072]{1,0:T(8,128)(2,1)S(1)}, u32[]{:S(2)}, u32[]{:S(2)}) collective-permute-start(bf16[6,3072]{1,0:T(8,128)(2,1)S(1)} %slice.79), channel_id=1, source_target_pairs={{8,0},{16,8},{24,16},{32,24},{40,32},{48,40},{56,48},{64,56},{72,6... | collective-permute-start | bytes 110600 | tf_op jit(solution)/shard_map/ppermute | solution.py:13
  135.2 2.6 copy-start.11
  135.2 2.6 copy-start.13
  226.6 1.4 slice-start
Sparse Core Ops, SparseCore 0:
  129.7 224.4 all-reduce.2
where the time goes:
time: 367 us; the launch traced here: 365 us
  waiting for transfers between devices  127 us (35%)
  blocking collectives  82.3 us (22%)
  local copies, waits for them, and re-layouts  73.4 us (20%)
  matrix products  46.5 us (13%)
  between operations  16.3 us (4%)
  other arithmetic  10.8 us (3%)
  starting transfers between devices  8.5 us (2%)
    psum x1, waiting for transfers between devices, body(): long_all, short_all = lax.psum((long_local, short_local), 'ctx')  124 us
    pmax x1, blocking collectives, body(): peak = lax.pmax(local_peak, ('ctx', 'tp'))  82.3 us
    conv_general_dilated x4, matrix products, later_filter(): lax.conv_general_dilated(operand, kernel_in, (1,), 'VALID', dimension_num...  33.4 us
    conv_general_dilated x5, local copies, waits for them, and re-layouts, causal_filter(): lax.conv_general_dilated(operand, kernel_in, (1,), 'VALID', dimension_num...  17.8 us
    conv_general_dilated x2, matrix products, causal_filter(): lax.conv_general_dilated(operand, kernel_in, (1,), 'VALID', dimension_num...  13.1 us
    unnamed x36, local copies, waits for them, and re-layouts  12.8 us
    broadcast_in_dim x2, local copies, waits for them, and re-layouts, later_filter(): operand = extended[None]  9.29 us
    ppermute x3, starting transfers between devices, shifted(): lax.ppermute(value, axis, [(source, source + steps) for source in range(l...  8.46 us
  transfers between devices with their start and end apart: 4, of which 2 were waited for; matrix products, arithmetic and copies ran while one was open for 16% of the time, Pallas kernels for 0%

commit v1 on v0

v1 whole, which is shorter than its diff:
```python
import functools

import jax
import jax.numpy as jnp
import ml_dtypes
import numpy as np
from jax import lax
from jax.experimental import pallas as pl
from jax.experimental.pallas import tpu as pltpu
from jax.sharding import PartitionSpec as P

EPSILON = 1e-06
FP8_RANGE = 448.0
MESH = pl.DeviceIdType.MESH

HALF = 208
SIZE = 2 * HALF
EDGE = 144
NEAR = 16
GROUP = 256
TILES = GROUP // 128
SPAN = 392
CHUNK = 56
BLOCKS = HALF // 16
f32 = jnp.float32
bf16 = jnp.bfloat16


def split_np(matrix):
    high = matrix.astype(ml_dtypes.bfloat16)
    low = (matrix - high.astype(np.float64)).astype(ml_dtypes.bfloat16)
    return high, low


def joined_np(matrix):
    high, low = split_np(matrix)
    return np.concatenate([high, high, low], axis=1)


@functools.lru_cache(None)
def transforms():
    m = np.arange(HALF)[None, :]
    k = np.arange(HALF // 2)[:, None]
    even_re = np.cos(2 * np.pi * ((k * m) % HALF) / HALF)
    even_im = -np.sin(2 * np.pi * ((k * m) % HALF) / HALF)
    even_im[0] = np.cos(np.pi * m[0])
    odd_re = np.cos(2 * np.pi * (((2 * k + 1) * m) % SIZE) / SIZE)
    odd_im = -np.sin(2 * np.pi * (((2 * k + 1) * m) % SIZE) / SIZE)

    def blocks(re, im):
        return np.stack([re.reshape(BLOCKS, 8, HALF), im.reshape(BLOCKS, 8, HALF)], axis=1).reshape(HALF, HALF)

    even = blocks(even_re, even_im)
    odd = blocks(odd_re, odd_im)
    weight = np.full((HALF // 2, 1), 2.0 / SIZE)
    first = weight.copy()
    first[0] = 1.0 / SIZE
    back_even = blocks(even_re * first, even_im * first).T
    back_odd = blocks(odd_re * weight, odd_im * weight).T
    c = np.arange(128)
    core, x, z, r = c // 64, (c // 32) % 2, (c // 4) % 8, c % 4
    lag = 128 - ((z * 4 + x * 2 + core) * 4 + r)
    back_lag = np.concatenate([back_even[lag % HALF], back_odd[lag % HALF]], axis=1)
    both = np.concatenate([even, odd], axis=0)
    ahead = np.concatenate([even, -odd], axis=0)[:, 48 : 48 + EDGE]
    return (
        joined_np(even),
        joined_np(odd),
        joined_np(both[:, :128]),
        joined_np(ahead),
        joined_np(back_even),
        joined_np(back_odd),
        joined_np(back_lag),
    )


def split(value):
    high = value.astype(bf16)
    low = (value - high.astype(f32)).astype(bf16)
    return high, low


def dot(a, b):
    return lax.dot_general(a, b, (((1,), (0,)), ((), ())), preferred_element_type=f32)


def main_kernel(
    x_hbm, g_hbm, sf_hbm, lf_hbm, fe_h, fo_h, fh_h, fa_h, be_h, bo_h, bl_h,
    din_hbm, lout, sout, pout,
    x_own, g_own, pkv, pq, nq, ng, nkv, sf, lf, fe, fo, fh, fa, be, bo, bl,
    xs, gs, kf, vf, ps, ds, hi, lo, sp, sd, sx, sh, er, orr, fil, dpr, df,
    din, lgs, sgs, lb1, sb1, lb2, sb2, zsrc, zbuf, szbuf, pbuf1, pbuf2, pbuf3, pone, ptwo, pthree,
    loads, own, stores, halo_s, halo_r, core_s, core_r, x_s, x_r, epi_s, epi_r,
):
    me = lax.axis_index("ctx")
    count = lax.axis_size("ctx")
    tp = lax.axis_index("tp")
    after = {"ctx": lax.rem(me + 1, count)}
    before = {"ctx": lax.rem(me + count - 1, count)}
    core = lax.rem(me, 2)
    x = lax.rem(me // 2, 2)
    z = me // 4
    hx = tp // 4
    y = lax.rem(tp, 4)
    rows = x_hbm.shape[1]
    groups = x_own.shape[0]

    def at(zz, xx, cc, hh, yy):
        return {"ctx": zz * 4 + xx * 2 + cc, "tp": hh * 4 + yy}

    pair = at(z, x, 1 - core, hx, y)
    cross = at(z, 1 - x, core, hx, y)
    diagonal = at(z, 1 - x, 1 - core, hx, y)
    rings = [at(lax.rem(z + n, 8), x, core, hx, y) for n in range(1, 8)]
    columns = [at(z, x, core, hx, lax.rem(y + n, 4)) for n in range(1, 4)]
    line = [
        at(z, (x + n // 2) % 2, (core + n) % 2, (hx + n // 4) % 2, y) for n in range(1, 8)
    ]
    barrier = pltpu.get_barrier_semaphore()
    for other in [after, before, *line, *columns, *rings]:
        pl.semaphore_signal(barrier, inc=1, device_id=other, device_id_type=MESH)

    def own_copies(i):
        lanes = pl.ds(pl.multiple_of(i * GROUP, GROUP), GROUP)
        return (
            pltpu.make_async_copy(x_hbm.at[:, :, lanes], x_own.at[i], own.at[0, i]),
            pltpu.make_async_copy(g_hbm.at[:, lanes], g_own.at[i], own.at[1, i]),
        )

    def halo_copies(i):
        lanes = pl.ds(pl.multiple_of(i * GROUP, GROUP), GROUP)
        plan = (
            (x_hbm.at[0, pl.ds(rows - NEAR, NEAR), lanes], pq.at[i], after),
            (x_hbm.at[pl.ds(1, 2), pl.ds(0, NEAR), lanes], nkv.at[i], before),
            (x_hbm.at[pl.ds(1, 2), pl.ds(rows - EDGE, EDGE), lanes], pkv.at[i], after),
            (x_hbm.at[0, pl.ds(0, EDGE), lanes], nq.at[i], before),
            (g_hbm.at[pl.ds(0, EDGE), lanes], ng.at[i], before),
        )
        return [
            pltpu.make_async_remote_copy(
                src_ref=source,
                dst_ref=target,
                send_sem=halo_s.at[n, i],
                recv_sem=halo_r.at[n, i],
                device_id=other,
                device_id_type=MESH,
            )
            for n, (source, target, other) in enumerate(plan)
        ]

    consts = [
        pltpu.make_async_copy(source, target, loads.at[n])
        for n, (source, target) in enumerate(
            ((sf_hbm, sf), (lf_hbm, lf), (fe_h, fe), (fo_h, fo), (fh_h, fh), (fa_h, fa), (be_h, be), (bo_h, bo), (bl_h, bl))
        )
    ]
    for copy in own_copies(0):
        copy.start()
    for copy in consts:
        copy.start()
    for i in range(1, groups):
        for copy in own_copies(i):
            copy.start()
    pl.semaphore_wait(barrier, 19)
    for i in range(groups):
        for copy in halo_copies(i):
            copy.start()
    for copy in consts:
        copy.wait()
    inner = (me > 0).astype(f32)
    outer = (me < count - 1).astype(f32)

    def remote(source, target, send, recv, other):
        return pltpu.make_async_remote_copy(
            src_ref=source, dst_ref=target, send_sem=send, recv_sem=recv, device_id=other, device_id_type=MESH
        )

    def core_copies(i):
        lanes = pl.ds(pl.multiple_of((1 - core) * 128, 128), 128)
        return (
            remote(
                lgs.at[i, pl.ds(pl.multiple_of((1 - core) * 64, 64), 64)], lb1.at[i], core_s.at[0, i], core_r.at[0, i], pair
            ),
            remote(sgs.at[i, :, lanes], sb1.at[i], core_s.at[1, i], core_r.at[1, i], pair),
        )

    def x_copies(i):
        return (
            remote(lb1.at[i, pl.ds(pl.multiple_of((1 - x) * 32, 32), 32)], lb2.at[i], x_s.at[i], x_r.at[i], cross),
        )

    def after_core(i):
        for copy in core_copies(i):
            copy.wait()
        lb1[i] = lb1[i] + lgs[i, pl.ds(pl.multiple_of(core * 64, 64), 64), :]
        sb1[i] = sb1[i] + sgs[i, :, pl.ds(pl.multiple_of(core * 128, 128), 128)]
        for copy in x_copies(i):
            copy.start()

    def group(i, top):
        for copy in own_copies(i):
            copy.wait()
        for copy in halo_copies(i):
            copy.wait_recv()
        for t in range(TILES):
            lanes = pl.ds(128 * t, 128)
            xs[0, t, 0:NEAR] = pq[i, :, lanes].astype(f32) * inner
            xs[0, t, NEAR : NEAR + 256] = x_own[i, 0, :, lanes].astype(f32)
            xs[0, t, NEAR + 256 : SIZE] = nq[i, :, lanes].astype(f32)
            for s in (1, 2):
                xs[s, t, 0:EDGE] = pkv[i, s - 1, :, lanes].astype(f32) * inner
                xs[s, t, EDGE : EDGE + 256] = x_own[i, s, :, lanes].astype(f32)
                xs[s, t, EDGE + 256 : SIZE] = nkv[i, s - 1, :, lanes].astype(f32)
            gs[t, 0:256] = g_own[i, :, lanes].astype(f32)
            gs[t, 256 : 256 + EDGE] = ng[i, :, lanes].astype(f32) * outer
            ps[t, SPAN:SIZE] = jnp.zeros((SIZE - SPAN, 128), f32)
            ds[t, SPAN:SIZE] = jnp.zeros((SIZE - SPAN, 128), f32)

        def tap(s, n, t):
            lanes = pl.ds(pl.multiple_of(i * GROUP + 128 * t, 128), 128)
            return sf[s, n : n + 1, lanes]

        for t in range(TILES):

            def features(c, _, t=t):
                base = pl.multiple_of(c * CHUNK, 8)
                parts = []
                for s in range(3):
                    total = None
                    for n in range(7):
                        term = xs[s, t, pl.ds(base + NEAR - n, CHUNK), :] * tap(s, n, t)
                        total = term if total is None else total + term
                    parts.append(total)
                here = pl.ds(base, CHUNK)
                kf[t, here, :] = parts[1]
                vf[t, here, :] = parts[2]
                ps[t, here, :] = parts[1] * parts[2]
                ds[t, here, :] = parts[0] * gs[t, here, :]
                return 0

            lax.fori_loop(0, SPAN // CHUNK, features, 0)

        def rows_of(ref, start, size):
            return jnp.concatenate([ref[t, start : start + size, :] for t in range(TILES)], axis=1)

        def put(slot, start, value):
            high, low = split(value)
            hi[slot, start : start + value.shape[0], :] = high
            lo[slot, start : start + value.shape[0], :] = low

        def taken(slot, size=HALF):
            high = hi[slot, 0:size, :]
            return jnp.concatenate([high, lo[slot, 0:size, :], high], axis=0)

        for b in range(BLOCKS):
            low_rows, high_rows = rows_of(ps, 16 * b, 16), rows_of(ps, HALF + 16 * b, 16)
            put(0, 16 * b, low_rows + high_rows)
            put(1, 16 * b, low_rows - high_rows)
            low_rows = rows_of(ds, 16 * b, 16)
            if b < 3:
                high_rows = rows_of(ds, HALF + 16 * b, 16)
                put(2, 16 * b, low_rows + high_rows)
                put(3, 16 * b, low_rows - high_rows)
            else:
                put(2, 16 * b, low_rows)
        for b in range(EDGE // 16):
            put(4, 16 * b, rows_of(ds, 256 + 16 * b, 16))
        for b in range(8):
            put(5, 16 * b, lf[16 * b : 16 * b + 16, pl.ds(pl.multiple_of(i * GROUP, GROUP), GROUP)])
        hi[3, 48:HALF, :] = hi[2, 48:HALF, :]
        lo[3, 48:HALF, :] = lo[2, 48:HALF, :]
        sh[...] = dot(fh[...], taken(5, 128))
        sp[0:HALF] = dot(fe[...], taken(0))
        sp[HALF:SIZE] = dot(fo[...], taken(1))
        sd[0:HALF] = dot(fe[...], taken(2))
        sd[HALF:SIZE] = dot(fo[...], taken(3))
        sx[...] = sd[...] + dot(fa[...], taken(4, EDGE))

        row = lax.broadcasted_iota(jnp.int32, (8, GROUP), 0)
        for part in range(2):
            for b in range(BLOCKS):
                start = HALF * part + 16 * b

                def two(ref, start=start):
                    return ref[start : start + 8, :], ref[start + 8 : start + 16, :]

                pr, pi = two(sp)
                hr, him = two(sh)
                dr, di = two(sd)
                xr, xi = two(sx)
                special = part == 0 and b == 0

                def pack(same, cross_, re, im, sign, special=special):
                    if special:
                        real = re + sign * jnp.where(row == 0, 0.0, same)
                        imag = jnp.where(row == 0, same, im + cross_)
                    else:
                        real = re + same if sign > 0 else re - same
                        imag = im + cross_
                    return jnp.concatenate([real, imag], axis=0)

                put(part, 16 * b, pack(pi * him, pi * hr, pr * hr, pr * him, -1.0))
                put(2 + part, 16 * b, pack(xi * him, xi * hr, xr * hr, -(xr * him), 1.0))
                put(4 + part, 16 * b, pack(di * pi, -(di * pr), dr * pr, dr * pi, 1.0))

        high = jnp.concatenate([hi[4, 0:HALF, :], hi[5, 0:HALF, :]], axis=0)
        low = jnp.concatenate([lo[4, 0:HALF, :], lo[5, 0:HALF, :]], axis=0)
        lgs[i] = dot(bl[...], jnp.concatenate([high, low, high], axis=0))
        er[0] = dot(be[...], taken(0))
        orr[0] = dot(bo[...], taken(1))
        er[1] = dot(be[...], taken(2))
        orr[1] = dot(bo[...], taken(3))

        for t in range(TILES):
            lanes = pl.ds(128 * t, 128)
            fil[t, 0:80, :] = er[0, 128:HALF, lanes] + orr[0, 128:HALF, lanes]
            fil[t, 80:264, :] = er[0, 0:184, lanes] - orr[0, 0:184, lanes]
            dpr[t, 0:HALF, :] = er[1, :, lanes] + orr[1, :, lanes]
            dpr[t, HALF:264, :] = er[1, 0:56, lanes] - orr[1, 0:56, lanes]
            df[0, t, 0:264, :] = gs[t, 0:264, :] * fil[t]
            df[1, t, 0:264, :] = dpr[t] * vf[t, 128:SPAN, :]
            df[2, t, 0:264, :] = dpr[t] * kf[t, 128:SPAN, :]

        for t in range(TILES):
            lanes = pl.ds(128 * t, 128)
            for s in range(3):
                shift = NEAR if s == 0 else EDGE

                def step(c, carry, s=s, t=t, lanes=lanes, shift=shift):
                    top, sums = carry
                    base = pl.multiple_of(c * 64, 8)
                    total = None
                    for n in range(7):
                        term = df[s, t, pl.ds(base + n, 64), :] * tap(s, n, t)
                        total = term if total is None else total + term
                    din[i, s, pl.ds(base, 64), lanes] = total
                    top = jnp.maximum(top, jnp.max(jnp.abs(total).reshape(8, 8, 128), axis=0))
                    here = df[s, t, pl.ds(base, 64), :]
                    new = []
                    for n in range(7):
                        term = here * xs[s, t, pl.ds(base + shift - n, 64), :]
                        new.append(sums[n] + jnp.sum(term.reshape(8, 8, 128), axis=0))
                    return top, tuple(new)

                zero = jnp.zeros((8, 128), f32)
                top, sums = lax.fori_loop(0, 4, step, (top, (zero,) * 7))
                sgs[i, 8 * s : 8 * s + 8, lanes] = jnp.concatenate(
                    [jnp.sum(v, axis=0, keepdims=True) for v in sums] + [jnp.zeros((1, 128), f32)], axis=0
                )
        din_copy(i).start()
        for copy in core_copies(i):
            copy.start()

        @pl.when(i > 0)
        def _():
            after_core(i - 1)

        return top

    def din_copy(i):
        lanes = pl.ds(pl.multiple_of(i * GROUP, GROUP), GROUP)
        return pltpu.make_async_copy(din.at[i], din_hbm.at[:, :, lanes], stores.at[i])

    top = lax.fori_loop(0, groups, group, jnp.zeros((8, 128), f32))

    pone[...] = top
    tops = [remote(pone, pbuf1.at[n], epi_s.at[n], epi_r.at[n], other) for n, other in enumerate(line)]
    for copy in tops:
        copy.start()
    after_core(groups - 1)
    for copy in tops:
        copy.wait()
    for n in range(7):
        top = jnp.maximum(top, pbuf1[n])
    ptwo[...] = top
    tops = [remote(ptwo, pbuf2.at[n], epi_s.at[7 + n], epi_r.at[7 + n], other) for n, other in enumerate(columns)]
    for copy in tops:
        copy.start()
    half = remote(sb1.at[pl.ds(pl.multiple_of((1 - x) * 2, 2), 2)], sb2, epi_s.at[10], epi_r.at[10], cross)
    half.start()
    for i in range(groups):
        for copy in x_copies(i):
            copy.wait()
        total = lb2[i] + lb1[i, pl.ds(pl.multiple_of(x * 32, 32), 32), :]
        for n in range(8):
            zsrc[n, :, GROUP * i : GROUP * (i + 1)] = total[4 * n : 4 * n + 4, :]
    for copy in tops:
        copy.wait()
    for n in range(3):
        top = jnp.maximum(top, pbuf2[n])
    pthree[...] = top
    tops = [remote(pthree, pbuf3.at[n], epi_s.at[11 + n], epi_r.at[11 + n], other) for n, other in enumerate(rings)]
    for copy in tops:
        copy.start()
    half.wait()
    two_x = pl.ds(pl.multiple_of(x * 2, 2), 2)
    mine = sb2[...] + sb1[two_x]
    sb2[...] = mine
    longs = [
        remote(zsrc.at[lax.rem(z + n + 1, 8)], zbuf.at[n], epi_s.at[18 + n], epi_r.at[18 + n], rings[n]) for n in range(7)
    ]
    shorts = [remote(sb2, szbuf.at[n], epi_s.at[25 + n], epi_r.at[25 + n], rings[n]) for n in range(7)]
    for copy in (*shorts, *longs):
        copy.start()
    for copy in tops:
        copy.wait()
    for n in range(7):
        top = jnp.maximum(top, pbuf3[n])
    pout[...] = top
    for copy in shorts:
        copy.wait()
    for n in range(7):
        mine = mine + szbuf[n]
    sout[core, two_x] = mine
    quarter = sout.at[core, two_x]
    lasts = [
        remote(quarter, quarter, epi_s.at[32 + n], epi_r.at[32 + n], other)
        for n, other in enumerate((pair, cross, diagonal))
    ]
    for copy in lasts:
        copy.start()
    for copy in longs:
        copy.wait()
    whole = zsrc[z]
    for n in range(7):
        whole = whole + zbuf[n]
    lout[...] = whole
    for i in range(groups):
        for copy in halo_copies(i):
            copy.wait_send()
        din_copy(i).wait()
    for copy in lasts:
        copy.wait()


def main(x3, cotangent, sf, lf):
    _, rows, chan = x3.shape
    consts = [jnp.asarray(c) for c in transforms()]
    groups = chan // GROUP
    anywhere = pl.BlockSpec(memory_space=pl.ANY)
    vmem = pl.BlockSpec(memory_space=pltpu.VMEM)
    V = pltpu.VMEM
    D = pltpu.SemaphoreType.DMA
    return pl.pallas_call(
        main_kernel,
        out_shape=[
            jax.ShapeDtypeStruct((3, rows, chan), f32),
            jax.ShapeDtypeStruct((4, chan), f32),
            jax.ShapeDtypeStruct((2, groups, 24, 128), f32),
            jax.ShapeDtypeStruct((8, 128), f32),
        ],
        in_specs=[anywhere] * (4 + len(consts)),
        out_specs=[anywhere, vmem, vmem, vmem],
        scratch_shapes=[
            V((groups, 3, rows, GROUP), bf16),
            V((groups, rows, GROUP), bf16),
            V((groups, 2, EDGE, GROUP), bf16),
            V((groups, NEAR, GROUP), bf16),
            V((groups, EDGE, GROUP), bf16),
            V((groups, EDGE, GROUP), bf16),
            V((groups, 2, NEAR, GROUP), bf16),
            V(sf.shape, f32),
            V(lf.shape, f32),
            *[V(c.shape, bf16) for c in consts],
            V((3, TILES, SIZE, 128), f32),
            V((TILES, 256 + EDGE, 128), f32),
            V((TILES, SPAN, 128), f32),
            V((TILES, SPAN, 128), f32),
            V((TILES, SIZE, 128), f32),
            V((TILES, SIZE, 128), f32),
            V((6, HALF, GROUP), bf16),
            V((6, HALF, GROUP), bf16),
            V((SIZE, GROUP), f32),
            V((SIZE, GROUP), f32),
            V((SIZE, GROUP), f32),
            V((SIZE, GROUP), f32),
            V((2, HALF, GROUP), f32),
            V((2, HALF, GROUP), f32),
            V((TILES, 264, 128), f32),
            V((TILES, 264, 128), f32),
            V((3, TILES, 272, 128), f32),
            V((groups, 3, rows, GROUP), f32),
            V((groups, 128, GROUP), f32),
            V((groups, 24, GROUP), f32),
            V((groups, 64, GROUP), f32),
            V((groups, 24, 128), f32),
            V((groups, 32, GROUP), f32),
            V((groups // 2, 24, 128), f32),
            V((8, 4, chan), f32),
            V((7, 4, chan), f32),
            V((7, groups // 2, 24, 128), f32),
            V((7, 8, 128), f32),
            V((3, 8, 128), f32),
            V((7, 8, 128), f32),
            V((8, 128), f32),
            V((8, 128), f32),
            V((8, 128), f32),
            D((9,)),
            D((2, groups)),
            D((groups,)),
            D((5, groups)),
            D((5, groups)),
            D((2, groups)),
            D((2, groups)),
            D((groups,)),
            D((groups,)),
            D((35,)),
            D((35,)),
        ],
        compiler_params=pltpu.CompilerParams(
            collective_id=0, has_side_effects=True, vmem_limit_bytes=56 * 1024 * 1024
        ),
        name="gradients",
    )(x3, cotangent, sf, lf, *consts)


def scale_kernel(din, peak, out, scale):
    top = jnp.max(peak[...]) + EPSILON
    out[...] = (din[...] * (FP8_RANGE / top)).astype(bf16)
    scale[0, 0] = top / FP8_RANGE


def scaled(din, peak):
    _, rows, chan = din.shape
    return pl.pallas_call(
        scale_kernel,
        grid=(4,),
        out_shape=[jax.ShapeDtypeStruct((3, rows, chan), bf16), jax.ShapeDtypeStruct((1, 1), f32)],
        in_specs=[
            pl.BlockSpec((3, rows // 4, chan), lambda i: (0, i, 0)),
            pl.BlockSpec((8, 128), lambda i: (0, 0)),
        ],
        out_specs=[
            pl.BlockSpec((3, rows // 4, chan), lambda i: (0, i, 0)),
            pl.BlockSpec((1, 1), lambda i: (0, 0), memory_space=pltpu.SMEM),
        ],
        compiler_params=pltpu.CompilerParams(vmem_limit_bytes=56 * 1024 * 1024),
        name="scaling",
    )(din, peak)


def body(projected, cotangent, short_filter, long_filter):
    chan = projected.shape[2]
    x3 = projected.transpose(1, 0, 2)
    sf = short_filter.transpose(1, 0, 2)
    din, long_grad, short_all, top = main(x3, cotangent, sf, long_filter)
    out, scale = scaled(din, top)
    parts = short_all.reshape(2, chan // GROUP, 3, 8, 128)[:, :, :, :7]
    short_grad = parts.transpose(3, 2, 1, 0, 4).reshape(7, 3, chan)
    return out.transpose(1, 0, 2), long_grad, short_grad, scale.reshape(())


def solution(mesh):
    placed = (P("ctx", None, "tp"), P("ctx", "tp"), P(None, None, "tp"), P(None, "tp"))
    return jax.shard_map(
        body,
        mesh=mesh,
        in_specs=placed,
        out_specs=(P("ctx", None, "tp"), P("ctx", "tp"), P(None, None, "tp"), P()),
        check_vma=False,
    )
```

time: 367 us -> 59.9 us (0.16)
  the two profiles are of different devices: /device:TPU:1 before, /device:TPU:5 now
where the time goes in v1:
time: 59.9 us; the launch traced here: 59.7 us
  Pallas kernels  57.6 us (96%)
  local copies, waits for them, and re-layouts  1.4 us (2%)
  between operations  0.67 us (1%)
    pallas_call x1, Pallas kernels, main(): pl.pallas_call(main_kernel, out_shape=[jax.ShapeDtypeStruct((3, rows, cha...  53.3 us
    pallas_call x1, Pallas kernels, scaled(): pl.pallas_call(scale_kernel, grid=(4,), out_shape=[jax.ShapeDtypeStruct((...  4.34 us

profile of v1, /device:TPU:5, one launch (start us, length us, event | category | flops | bytes accessed | tf_op | source)
XLA Modules:
  0.0 59.7 jit_solution(1221491169197820902)
XLA Ops:
  0.6 53.3 %gradients.1 = (f32[3,256,1024]{2,1,0:T(8,128)}, f32[4,1024]{1,0:T(4,128)}, f32[2,4,24,128]{3,2,1,0:T(8,128)}, f32[8,128]{1,0:T(8,128)}) custom-call(bf16[3,256,1024]{2,1,0:T(8,128)(2,1)} %bitcast.9, bf16[256,1024]{1,0:T(8,128)(2,1)} %g_hbm.1, f32[3,7,1024]{2,1,0:T(8,128)} %bitcast.11, f32[128,1024]{1,0:T(8,128)} %lf_hbm.1, ...), custom_call_target="tpu_custom_call" | custom-call | tf_op jit(solution)/shard_map/gradients/pallas_call | solution.py:444
  53.9 0.0 copy-start
  54.0 0.0 copy-start.1
  54.0 4.3 %scaling.1 = (bf16[3,256,1024]{2,1,0:T(8,128)(2,1)}, f32[1,1]{1,0:T(1,128)}) custom-call(f32[3,256,1024]{2,1,0:T(8,128)} %get-tuple-element.10.din, f32[8,128]{1,0:T(8,128)} %get-tuple-element.11.peak), custom_call_target="tpu_custom_call" | custom-call | tf_op jit(solution)/shard_map/scaling/pallas_call | solution.py:525
  58.3 0.0 copy-done
  58.3 0.1 copy.15
  58.4 0.7 %reshape.18 = f32[7,3,1024]{2,0,1:T(8,128)} reshape(f32[7,3,4,2,128]{4,3,2,0,1:T(2,128)S(1)} %copy.15) | data formatting | bytes 172032 | tf_op jit(solution)/shard_map/reshape | solution.py:549
  59.1 0.0 copy-done.1
  59.1 0.6 %copy.17 = f32[4,1024]{1,0:T(4,128)} copy(f32[4,1024]{1,0:T(4,128)S(1)} %copy-done.1) | data formatting | bytes 32768
  (1 shorter events, 0.0 us)
Async XLA Ops:
  53.9 4.4 %copy-start = (f32[2,4,24,128]{3,2,1,0:T(8,128)S(1)}, f32[2,4,24,128]{3,2,1,0:T(8,128)}, u32[]{:S(2)}) copy-start(f32[2,4,24,128]{3,2,1,0:T(8,128)} %get-tuple-element.14) | copy-start | bytes 294916
  54.0 5.1 %copy-start.1 = (f32[4,1024]{1,0:T(4,128)S(1)}, f32[4,1024]{1,0:T(4,128)}, u32[]{:S(2)}) copy-start(f32[4,1024]{1,0:T(4,128)} %get-tuple-element.21) | copy-start | bytes 49156
